TPU v7x, 512 devices: a whole 4x4x16 slice. The times are simulated.
512 devices in a mesh: inst: 32 (over x_hi, z), tp: 16 (over x_lo, y, core).
Axes of the slice: x: 4 (x_hi: 2, x_lo: 2; x = x_hi * 2 + x_lo), y: 4, z: 16, core: 2. Of those that a mesh axis runs over, the one named last changes fastest.
Arguments:
- kv_pool: bfloat16 [1792, 16, 2, 128, 128], P('inst', 'tp'), may hold values from -4 to 4, as said below
- block_table: int32 [192, 8], P('inst'), may hold values from 0 to 55, as said below
- mig_table: int32 [32, 8], P('inst'), may hold values from 0 to 55, as said below
- query_stay: bfloat16 [192, 8192], P('inst', 'tp'), may hold values from -8 to 8
- query_mig: bfloat16 [32, 8192], P('inst', 'tp'), may hold values from -8 to 8
- new_stay: bfloat16 [192, 16, 2, 128], P('inst', 'tp'), may hold values from -4 to 4, as said below
- new_mig: bfloat16 [32, 16, 2, 128], P('inst', 'tp'), may hold values from -4 to 4, as said below
- len_stay: int32 [192], P('inst'), may hold values from 1 to 1024, as said below
- len_mig: int32 [32], P('inst'), may hold values from 1 to 1024, as said below
- hidden_stay: bfloat16 [192, 8192], P('inst', 'tp'), may hold values from -60 to 60
- hidden_mig: bfloat16 [32, 8192], P('inst', 'tp'), may hold values from -60 to 60
- norm_gain: bfloat16 [8192], P('tp'), may hold values from 0.099609375 to 1.8984375
- partner_mask: int32 [1], replicated, may hold values from 1 to 31
Outputs:
- attended: bfloat16 [224, 8192], P('inst', 'tp')
- arrived_pages: bfloat16 [32, 8, 16, 2, 128, 128], P('inst', None, 'tp')
- normed: bfloat16 [224, 8192], P('inst', 'tp')
Inputs may be any that keep to these rules, and one draw needn't show every extreme that they name: Each instance's block_table and mig_table rows together name each of its 56 local pages exactly once. `mig_table`: local page numbers, as in block_table. `len_stay`: lengths count cached tokens with the new one. `len_mig`: lengths count cached tokens with the new one. `kv_pool`: slot s holds kv head s // 2; slots of one head are equal. `new_stay`: slots of one kv head are equal. `new_mig`: slots of one kv head are equal. Instance i is matched with instance i XOR partner_mask[0].
All inputs are finite; a program needn't handle non-finite values.
Results may differ from a plain program's by a relative error of at most 0.0047.
Values may be sent and summed in bfloat16 or wider, within the bound.
A program may use at most 64 MiB of HBM per device.

v0:
```python
import functools

import jax
import jax.numpy as jnp
from jax import lax
from jax.experimental import pallas as pl
from jax.experimental.pallas import tpu as pltpu
from jax.sharding import PartitionSpec as P

MESH = pl.DeviceIdType.MESH
D = 8192
LANES = 128
GROUP = 4
PAGES = 8
FIRST, SECOND = 1, 4
PARTS = 1
STEPS = ((1, 8, 9), (2, 4, 6))


def flipped(index, mask):
    bit = 1
    total = index
    while bit <= mask:
        if mask & bit:
            total = total + bit - 2 * bit * ((index // bit) % 2)
        bit *= 2
    return total


def greets_first(tp, bits):
    top = 1 << (bits.bit_length() - 1)
    side = tp // top % 2
    return side if bits == 1 else 1 - side


def attend(pool, page_of, query, new_kv, length):
    page = pool.shape[2]
    places = [page_of(j) for j in range(PAGES)]
    new_key = new_kv[0:1].astype(jnp.float32)
    new_value = new_kv[1:2].astype(jnp.float32)
    scale = LANES ** (-0.5)
    new_score = jnp.sum(query.astype(jnp.float32) * new_key, axis=1, keepdims=True) * scale
    column = lax.broadcasted_iota(jnp.int32, (query.shape[0], page), 1)
    scores = []
    for j, place in enumerate(places):
        score = lax.dot_general(
            query, pool[place, 0], (((1,), (1,)), ((), ())), preferred_element_type=jnp.float32
        )
        score = score * scale
        position = column + j * page
        score = jnp.where(position == length - 1, new_score, score)
        scores.append(jnp.where(position < length, score, -1e30))
    highest = functools.reduce(jnp.maximum, scores)
    highest = jnp.max(highest, axis=1, keepdims=True)
    weights = [
        jnp.where(column + j * page < length, jnp.exp(s - highest), 0.0)
        for j, s in enumerate(scores)
    ]
    total = jnp.sum(functools.reduce(jnp.add, weights), axis=1, keepdims=True)
    mixed = jnp.zeros((query.shape[0], LANES), jnp.float32)
    last = jnp.zeros((query.shape[0], page), jnp.float32)
    for j, (w, place) in enumerate(zip(weights, places)):
        w = (w / total).astype(jnp.bfloat16).astype(jnp.float32)
        is_last = column + j * page == length - 1
        last = last + jnp.where(is_last, w, 0.0)
        w = jnp.where(is_last, 0.0, w).astype(jnp.bfloat16)
        mixed = mixed + jnp.dot(w, pool[place, 1], preferred_element_type=jnp.float32)
    return mixed + jnp.sum(last, axis=1, keepdims=True) * new_value


def kernel(
    mask,
    kv_hbm,
    block_table_hbm,
    mig_table_hbm,
    len_stay_hbm,
    len_mig_hbm,
    query_stay_hbm,
    query_mig_hbm,
    new_stay_hbm,
    new_mig_hbm,
    hidden_stay_hbm,
    hidden_mig_hbm,
    gain_hbm,
    attended,
    arrived,
    normed,
    pool,
    block_table,
    mig_table,
    len_stay,
    len_mig,
    query_stay,
    query_mig,
    new_lines,
    hidden_stay,
    hidden_mig,
    gain,
    out_pages,
    queries,
    mixed,
    rows,
    sums_out,
    sums_in,
    note_out,
    note_in,
    pool_sem,
    load_sem,
    page_send,
    page_recv,
    pass_send,
    pass_recv,
    sum_send,
    sum_recv,
    note_send,
    note_recv,
    answer_sem,
):
    inst, tp = lax.axis_index("inst"), lax.axis_index("tp")
    core = tp % 2
    other = flipped(tp, 1)
    partner = flipped(inst, mask)
    stay = query_stay.shape[0]
    page_count, _, page, _ = pool.shape
    half = out_pages.shape[0]

    barrier = pltpu.get_barrier_semaphore()
    pl.semaphore_signal(barrier, inc=1, device_id=(partner, tp), device_id_type=MESH)
    others = STEPS[0] + STEPS[1]
    far = mask % 16 >= 4
    answers = 0
    for bits in others:
        first = greets_first(tp, bits) if far else 1
        answers = answers + first

        @pl.when(first == 1)
        def _(bits=bits):
            pl.semaphore_signal(
                barrier, inc=1, device_id=(inst, flipped(tp, bits)), device_id_type=MESH
            )

    part = page_count // PARTS
    pool_loads = [
        pltpu.make_async_copy(
            kv_hbm.at[pl.ds(c * part, part), 0], pool.at[pl.ds(c * part, part)], pool_sem.at[c]
        )
        for c in range(PARTS)
    ]
    pairs = [
        (hidden_stay_hbm, hidden_stay),
        (hidden_mig_hbm, hidden_mig),
        (mig_table_hbm, mig_table),
        (len_mig_hbm, len_mig),
        (new_mig_hbm.at[:, 0], new_lines.at[pl.ds(stay, 1)]),
        (query_stay_hbm, query_stay),
        (query_mig_hbm, query_mig),
        (block_table_hbm, block_table),
        (len_stay_hbm, len_stay),
        (new_stay_hbm.at[:, 0], new_lines.at[pl.ds(0, stay)]),
        (gain_hbm, gain),
    ]
    small_loads = [
        pltpu.make_async_copy(src, dst, load_sem.at[c]) for c, (src, dst) in enumerate(pairs)
    ]
    for load in small_loads[:5]:
        load.start()
    for load in pool_loads:
        load.start()
    for load in small_loads[5:]:
        load.start()

    rows[...] = jnp.zeros_like(rows)
    for load in small_loads[:2]:
        load.wait()
    rows[0:stay, :] = hidden_stay[...].astype(jnp.float32)
    rows[stay : stay + 1, :] = hidden_mig[...].astype(jnp.float32)
    square = rows[...] * rows[...]
    width = square.shape[1]
    sums_out[0] = sum(square[:, c : c + LANES] for c in range(0, width, LANES))

    def sum_copies(step):
        return [
            pltpu.make_async_remote_copy(
                src_ref=sums_out.at[step],
                dst_ref=sums_in.at[step, c],
                send_sem=sum_send.at[step, c],
                recv_sem=sum_recv.at[step, c],
                device_id=(inst, flipped(tp, bits)),
                device_id_type=MESH,
            )
            for c, bits in enumerate(STEPS[step])
        ]

    def summed(step):
        copies = sum_copies(step)
        for copy in copies:
            copy.wait()
        return sums_out[step] + sum(sums_in[step, c] for c in range(len(copies)))

    def page_copy(j):
        return pltpu.make_async_remote_copy(
            src_ref=out_pages.at[j],
            dst_ref=arrived.at[0, core * half + j, 0],
            send_sem=page_send.at[j],
            recv_sem=page_recv.at[j],
            device_id=(partner, tp),
            device_id_type=MESH,
        )

    def start_sums(step):
        for copy in sum_copies(step):
            copy.start()

    if far:
        pl.semaphore_wait(barrier, 1 + len(others) - answers)
        for bits in others:

            @pl.when(greets_first(tp, bits) == 0)
            def _(bits=bits):
                pl.semaphore_signal(
                    answer_sem, inc=1, device_id=(inst, flipped(tp, bits)), device_id_type=MESH
                )

    else:
        pl.semaphore_wait(barrier, 1 + len(others))
        start_sums(0)

    for load in small_loads[2:5] + pool_loads:
        load.wait()
    length = len_mig[0]
    new_line = new_lines[stay]
    position = lax.broadcasted_iota(jnp.int32, (page, LANES), 0)

    def send_page(j, _):
        at = mig_table[0, core * half + j]
        here = position == length - 1 - (core * half + j) * page
        for k in range(2):
            out_pages[j, k] = jnp.where(here, new_line[k : k + 1], pool[at, k])
        page_copy(j).start()
        return 0

    held = half * (inst // 4 % 2) if mask // 4 % 4 == 2 else 0
    lax.fori_loop(0, half - held, send_page, 0)
    if far:

        @pl.when(answers > 0)
        def _():
            pl.semaphore_wait(answer_sem, answers)

        start_sums(0)

    for load in small_loads[5:]:
        load.wait()
    queries[...] = jnp.zeros_like(queries)
    stay_q, mig_q = query_stay[...].astype(jnp.float32), query_mig[...].astype(jnp.float32)
    for h in range(GROUP):
        queries[0:stay, h, :] = stay_q[:, h * LANES : (h + 1) * LANES]
        queries[stay, h : h + 1, :] = mig_q[:, h * LANES : (h + 1) * LANES]

    own = stay
    note = pltpu.make_async_remote_copy(
        src_ref=note_out,
        dst_ref=note_in,
        send_sem=note_send,
        recv_sem=note_recv,
        device_id=(partner, tp),
        device_id_type=MESH,
    )

    def attend_next(i, _):
        r = own - i
        staying = jnp.minimum(r, stay - 1)

        def page_of(j):
            return jnp.where(r == own, mig_table[0, j], block_table[staying, j])

        mixed[r] = attend(
            pool,
            page_of,
            queries[r].astype(jnp.bfloat16),
            new_lines[r],
            jnp.where(r == own, length, len_stay[staying]),
        )

        @pl.when(i == 0)
        def _():
            if mask // 4 % 4 == 2:
                lax.fori_loop(half - held, half, send_page, 0)

        @pl.when(i == FIRST)
        def _():
            sums_out[1] = summed(0)
            start_sums(1)

        @pl.when(i == SECOND)
        def _():
            sums = summed(1)
            mean_square = jnp.sum(sums, axis=1, keepdims=True) / D
            scaled = rows[...] * lax.rsqrt(mean_square + 1e-05)
            rows[...] = scaled * gain[...].astype(jnp.float32)[None, :]
            line = rows[own : own + 1, :]
            lines = [line[:, h * LANES : (h + 1) * LANES] for h in range(GROUP)]
            note_out[0:8, :] = mixed[own].astype(jnp.bfloat16)
            note_out[8:16, :] = jnp.concatenate(lines + lines, axis=0).astype(jnp.bfloat16)
            note.start()

        return 0

    lax.fori_loop(0, stay + 1, attend_next, 0)

    def pass_copy(j):
        return pltpu.make_async_remote_copy(
            src_ref=arrived.at[0, core * half + j, 0],
            dst_ref=arrived.at[0, core * half + j, 0],
            send_sem=pass_send.at[j],
            recv_sem=pass_recv.at[j],
            device_id=(inst, other),
            device_id_type=MESH,
        )

    def pass_on(j, _):
        page_copy(j).wait_recv()
        pass_copy(j).start()
        return 0

    lax.fori_loop(0, half, pass_on, 0)

    note.wait()
    got = note_in[...].astype(jnp.float32)
    mixed[stay] = got[0:8]
    for h in range(GROUP):
        attended[:, h * LANES : (h + 1) * LANES] = mixed[:, h, :].astype(jnp.bfloat16)
        rows[stay : stay + 1, h * LANES : (h + 1) * LANES] = got[8 + h : 9 + h]
    normed[...] = rows[0 : stay + 1, :].astype(jnp.bfloat16)

    def finish(j, _):
        page_copy(j).wait_send()
        pass_copy(j).wait()
        return 0

    lax.fori_loop(0, half, finish, 0)


def settle(*refs):
    count = (len(refs) - 1) // 2
    copies = [
        pltpu.make_async_copy(refs[c], refs[count + c], refs[-1].at[c]) for c in range(count)
    ]
    for copy in copies:
        copy.start()
    for copy in copies:
        copy.wait()


def local(
    kv_pool,
    block_table,
    mig_table,
    query_stay,
    query_mig,
    new_stay,
    new_mig,
    len_stay,
    len_mig,
    hidden_stay,
    hidden_mig,
    norm_gain,
    partner_mask,
):
    page_count, _, _, page, head = kv_pool.shape
    stay, width = query_stay.shape
    slots = mig_table.shape[1]
    half = slots // 2
    bf16, f32 = jnp.bfloat16, jnp.float32
    vmem = pl.BlockSpec(memory_space=pltpu.VMEM)
    anywhere = pl.BlockSpec(memory_space=pl.ANY)
    dma = pltpu.SemaphoreType.DMA

    operands = (
        kv_pool,
        block_table,
        mig_table,
        len_stay,
        len_mig,
        query_stay,
        query_mig,
        new_stay,
        new_mig,
        hidden_stay,
        hidden_mig,
        norm_gain,
    )
    results = (
        jax.ShapeDtypeStruct((stay + 1, width), bf16),
        jax.ShapeDtypeStruct((1, slots, 1, 2, page, head), bf16),
        jax.ShapeDtypeStruct((stay + 1, width), bf16),
    )

    def matched(mask):
        return pl.pallas_call(
            functools.partial(kernel, mask),
            out_shape=results,
            in_specs=[anywhere] * len(operands),
            out_specs=(vmem, vmem, vmem),
            scratch_shapes=[
                pltpu.VMEM((page_count, 2, page, head), bf16),
                *(pltpu.SMEM(a.shape, a.dtype) for a in operands[1:5]),
                *(pltpu.VMEM(a.shape, a.dtype) for a in operands[5:7]),
                pltpu.VMEM((stay + 1, 2, head), bf16),
                *(pltpu.VMEM(a.shape, a.dtype) for a in operands[9:]),
                pltpu.VMEM((half, 2, page, head), bf16),
                pltpu.VMEM((stay + 1, 8, head), f32),
                pltpu.VMEM((stay + 1, 8, head), f32),
                pltpu.VMEM((8, width), f32),
                pltpu.VMEM((2, 8, LANES), f32),
                pltpu.VMEM((2, 3, 8, LANES), f32),
                pltpu.VMEM((16, LANES), bf16),
                pltpu.VMEM((16, LANES), bf16),
                dma((PARTS,)),
                dma((len(operands) - 1,)),
                dma((half,)),
                dma((half,)),
                dma((half,)),
                dma((half,)),
                dma((2, 3)),
                dma((2, 3)),
                dma,
                dma,
                pltpu.SemaphoreType.REGULAR,
            ],
            compiler_params=pltpu.CompilerParams(
                collective_id=mask - 1, has_side_effects=True, vmem_limit_bytes=32 * 1024 * 1024
            ),
            name="matched",
        )

    branches = [
        lambda *args, mask=mask: tuple(matched(mask)(*args))
        for mask in range(1, lax.axis_size("inst"))
    ]
    found = lax.switch(partner_mask[0] - 1, branches, *operands)
    return pl.pallas_call(
        settle,
        out_shape=results,
        in_specs=[vmem] * 3,
        out_specs=(anywhere,) * 3,
        scratch_shapes=[dma((3,))],
        compiler_params=pltpu.CompilerParams(vmem_limit_bytes=4 * 1024 * 1024),
        name="settle",
    )(*found)


def solution(mesh):
    return jax.shard_map(
        local,
        mesh=mesh,
        in_specs=(
            P("inst", "tp", None, None, None),
            P("inst", None),
            P("inst", None),
            P("inst", "tp"),
            P("inst", "tp"),
            P("inst", "tp", None, None),
            P("inst", "tp", None, None),
            P("inst"),
            P("inst"),
            P("inst", "tp"),
            P("inst", "tp"),
            P("tp"),
            P(),
        ),
        out_specs=(P("inst", "tp"), P("inst", None, "tp", None, None, None), P("inst", "tp")),
        check_vma=False,
    )
```

profile of v0, /device:TPU:33, one launch (start us, length us, event | category | flops | bytes accessed | tf_op | source)
XLA Modules:
  0.0 43.2 jit_solution(1934870855835999103)
XLA Ops:
  1.3 40.9 %conditional.1 = ((bf16[7,512]{1,0:T(8,128)(2,1)S(1)}, bf16[1,8,1,2,128,128]{5,4,3,2,1,0:T(8,128)(2,1)S(1)}, bf16[7,512]{1,0:T(8,128)(2,1)S(1)})) conditional(s32[]{:T(128)} %bitcast, (bf16[56,1,2,128,128]{4,3,2,1,0:T(8,128)(2,1)}, s32[6,8]{1,0:T(8,128)}, s32[1,8]{1,0:T(1,128)}, s32[6]{0:T(128)}, s32[1]{0:T(128)}, ...), branch_computations={%region_0.0_spmd, %region_1.0_spmd, %region_2.0_spmd, %region_3.0_... | conditional | bytes 8 | solution.py:441
  1.5 40.4 %matched.60 = (bf16[7,512]{1,0:T(8,128)(2,1)S(1)}, bf16[1,8,1,2,128,128]{5,4,3,2,1,0:T(8,128)(2,1)S(1)}, bf16[7,512]{1,0:T(8,128)(2,1)S(1)}) custom-call(bf16[56,1,2,128,128]{4,3,2,1,0:T(8,128)(2,1)} %get-tuple-element.1092.kv_hbm, s32[6,8]{1,0:T(8,128)} %get-tuple-element.1093.block_table_hbm, s32[1,8]{1,0:T(1,128)} %get-tuple-element.1094.mig_table_hbm, ...), custom_call_target="tpu_custom_call" | custom-call | tf_op jit(solution)/shard_map/cond/branch_29_fun/matched/pallas_call | solution.py:438
  42.1 0.8 %settle.1 = (bf16[7,512]{1,0:T(8,128)(2,1)}, bf16[1,8,1,2,128,128]{5,4,3,2,1,0:T(8,128)(2,1)}, bf16[7,512]{1,0:T(8,128)(2,1)}) custom-call(bf16[7,512]{1,0:T(8,128)(2,1)S(1)} %get-tuple-element.1122.refs_0_, bf16[1,8,1,2,128,128]{5,4,3,2,1,0:T(8,128)(2,1)S(1)} %get-tuple-element.1123.refs_1_, bf16[7,512]{1,0:T(8,128)(2,1)S(1)} %get-tuple-element.1124.refs_2_), custom_call_target="tpu_custom_call" | custom-call | tf_op jit(solution)/shard_map/settle/pallas_call | solution.py:442
where the time goes:
time: 43.3 us; the launch traced here: 43.2 us
  Pallas kernels  41.2 us (95%)
  between operations  1.47 us (3%)
  loops' own time  0.47 us (1%)
    pallas_call x1, Pallas kernels, local(): matched(mask)(*args)  40.4 us

commit v1 on v0

--- a/solution.py
+++ b/solution.py
@@ -124,21 +124,6 @@
     page_count, _, page, _ = pool.shape
     half = out_pages.shape[0]
 
-    barrier = pltpu.get_barrier_semaphore()
-    pl.semaphore_signal(barrier, inc=1, device_id=(partner, tp), device_id_type=MESH)
-    others = STEPS[0] + STEPS[1]
-    far = mask % 16 >= 4
-    answers = 0
-    for bits in others:
-        first = greets_first(tp, bits) if far else 1
-        answers = answers + first
-
-        @pl.when(first == 1)
-        def _(bits=bits):
-            pl.semaphore_signal(
-                barrier, inc=1, device_id=(inst, flipped(tp, bits)), device_id_type=MESH
-            )
-
     part = page_count // PARTS
     pool_loads = [
         pltpu.make_async_copy(
@@ -162,10 +147,25 @@
     small_loads = [
         pltpu.make_async_copy(src, dst, load_sem.at[c]) for c, (src, dst) in enumerate(pairs)
     ]
-    for load in small_loads[:5]:
+    for load in pool_loads + small_loads[:5]:
         load.start()
-    for load in pool_loads:
-        load.start()
+
+    barrier = pltpu.get_barrier_semaphore()
+    pl.semaphore_signal(barrier, inc=1, device_id=(partner, tp), device_id_type=MESH)
+    steps = STEPS[::-1] if mask in (17, 19) else STEPS
+    others = steps[0] + steps[1]
+    far = mask % 16 >= 4 or mask in (2, 3)
+    answers = 0
+    for bits in others:
+        first = greets_first(tp, bits) if far else 1
+        answers = answers + first
+
+        @pl.when(first == 1)
+        def _(bits=bits):
+            pl.semaphore_signal(
+                barrier, inc=1, device_id=(inst, flipped(tp, bits)), device_id_type=MESH
+            )
+
     for load in small_loads[5:]:
         load.start()
 
@@ -188,7 +188,7 @@
                 device_id=(inst, flipped(tp, bits)),
                 device_id_type=MESH,
             )
-            for c, bits in enumerate(STEPS[step])
+            for c, bits in enumerate(steps[step])
         ]
 
     def summed(step):

time: 43.3 us -> 38.6 us (0.89)
  the two profiles are of different devices: /device:TPU:33 before, /device:TPU:89 now
where the time goes in v1:
time: 38.6 us; the launch traced here: 38.4 us
  Pallas kernels  36.5 us (95%)
  between operations  1.47 us (4%)
  loops' own time  0.47 us (1%)
    pallas_call x1, Pallas kernels, local(): matched(mask)(*args)  35.6 us
    pallas_call x1, Pallas kernels, local(): pl.pallas_call(settle, out_shape=results, in_specs=[vmem] * 3, out_specs=...  0.83 us

profile of v1, /device:TPU:89, one launch (start us, length us, event | category | flops | bytes accessed | tf_op | source)
XLA Modules:
  0.0 38.4 jit_solution(7545972633515769880)
XLA Ops:
  1.3 36.1 %conditional.1 = ((bf16[7,512]{1,0:T(8,128)(2,1)S(1)}, bf16[1,8,1,2,128,128]{5,4,3,2,1,0:T(8,128)(2,1)S(1)}, bf16[7,512]{1,0:T(8,128)(2,1)S(1)})) conditional(s32[]{:T(128)} %bitcast, (bf16[56,1,2,128,128]{4,3,2,1,0:T(8,128)(2,1)}, s32[6,8]{1,0:T(8,128)}, s32[1,8]{1,0:T(1,128)}, s32[6]{0:T(128)}, s32[1]{0:T(128)}, ...), branch_computations={%region_0.0_spmd, %region_1.0_spmd, %region_2.0_spmd, %region_3.0_... | conditional | bytes 8 | solution.py:441
  1.3 35.6 %matched.52 = (bf16[7,512]{1,0:T(8,128)(2,1)S(1)}, bf16[1,8,1,2,128,128]{5,4,3,2,1,0:T(8,128)(2,1)S(1)}, bf16[7,512]{1,0:T(8,128)(2,1)S(1)}) custom-call(bf16[56,1,2,128,128]{4,3,2,1,0:T(8,128)(2,1)} %get-tuple-element.996.kv_hbm, s32[6,8]{1,0:T(8,128)} %get-tuple-element.997.block_table_hbm, s32[1,8]{1,0:T(1,128)} %get-tuple-element.998.mig_table_hbm, ...), custom_call_target="tpu_custom_call" | custom-call | tf_op jit(solution)/shard_map/cond/branch_21_fun/matched/pallas_call | solution.py:438
  37.4 0.8 %settle.1 = (bf16[7,512]{1,0:T(8,128)(2,1)}, bf16[1,8,1,2,128,128]{5,4,3,2,1,0:T(8,128)(2,1)}, bf16[7,512]{1,0:T(8,128)(2,1)}) custom-call(bf16[7,512]{1,0:T(8,128)(2,1)S(1)} %get-tuple-element.1122.refs_0_, bf16[1,8,1,2,128,128]{5,4,3,2,1,0:T(8,128)(2,1)S(1)} %get-tuple-element.1123.refs_1_, bf16[7,512]{1,0:T(8,128)(2,1)S(1)} %get-tuple-element.1124.refs_2_), custom_call_target="tpu_custom_call" | custom-call | tf_op jit(solution)/shard_map/settle/pallas_call | solution.py:442
